TPU v7x, 32 devices: a whole 2x2x4 slice. The times are simulated.
32 devices in a mesh: rc: 16 (over z, x, core), sys: 2 (over y).
Axes of the slice: x: 2, y: 2, z: 4, core: 2. Of those that a mesh axis runs over, the one named last changes fastest.
Arguments:
- density: bfloat16 [2, 64, 1600, 512], P(None, 'sys', 'rc'), may hold values from -6 to 6
- system_real: bfloat16 [64, 64], replicated, may hold values from -0.75 to 0.75
- system_imag: bfloat16 [64, 64], replicated, may hold values from -0.75 to 0.75
- left_ham: bfloat16 [40, 40], replicated, may hold values from -1 to 1
- left_coupling: bfloat16 [40, 40], replicated, may hold values from -1 to 1
- right_ham: bfloat16 [40, 40], replicated, may hold values from -1 to 1
- right_coupling: bfloat16 [40, 40], replicated, may hold values from -1 to 1
- left_strength: float32 [64], replicated, may hold values from -1.5 to 1.5
- right_strength: float32 [64], replicated, may hold values from -1.5 to 1.5
- left_damping: float32 [40], replicated, may hold values from 0.1 to 2
- right_damping: float32 [40], replicated, may hold values from 0.1 to 2
- energies: float32 [512], replicated, may hold values from -3 to 3
Outputs:
- derivative: bfloat16 [2, 64, 1600, 512], P(None, 'sys', 'rc')
All inputs are finite; a program needn't handle non-finite values.
Results may differ from a plain program's by a relative error of at most 0.0047.
Values may be sent and summed in bfloat16 or wider, within the bound.
A program may use at most 192 MiB of HBM per device.

v0:
```python
import math

import jax
import jax.numpy as jnp
from jax import lax
from jax.sharding import PartitionSpec as P


def symmetric(matrix, factor):
    widened = matrix.astype(jnp.float32)
    return ((widened + factor * widened.T) * 0.5).astype(jnp.bfloat16)


def ladder_local(regrouped, left_ops, right_ops, left_gain, right_gain, levels):
    item_count, group_count, all_pairs, column_count = regrouped.shape
    widened = regrouped.reshape(item_count, group_count, levels, levels * column_count)
    left_all = jnp.einsum("xa,ksam->ksxm", left_ops, widened, preferred_element_type=jnp.float32)
    left_term = left_all[:, :, :levels] + left_gain[None, :, None, None] * left_all[:, :, levels:]
    deepened = regrouped.reshape(item_count, group_count, levels, levels, column_count)
    right_all = jnp.einsum(
        "yb,ksabc->ksayc", right_ops, deepened, preferred_element_type=jnp.float32
    )
    right_term = (
        right_all[:, :, :, :levels]
        + right_gain[None, :, None, None, None] * right_all[:, :, :, levels:]
    )
    summed = left_term.reshape(
        item_count, group_count, all_pairs, column_count
    ) + right_term.reshape(item_count, group_count, all_pairs, column_count)
    return summed.astype(jnp.bfloat16)


def shards(
    density,
    system_real,
    system_imag,
    left_ham,
    left_coupling,
    right_ham,
    right_coupling,
    left_strength,
    right_strength,
    left_damping,
    right_damping,
    energies,
):
    herm_real = symmetric(system_real, 1.0)
    herm_imag = symmetric(system_imag, -1.0)
    levels = left_ham.shape[0]
    left_ops = jnp.concatenate([symmetric(left_ham, 1.0), symmetric(left_coupling, 1.0)], axis=0)
    right_ops = jnp.concatenate([symmetric(right_ham, 1.0), symmetric(right_coupling, 1.0)], axis=0)
    state_count = density.shape[1]
    pair_count = density.shape[2]
    column_total = density.shape[3]
    first_state = lax.axis_index("sys") * state_count
    left_gain = lax.dynamic_slice_in_dim(left_strength, first_state, state_count)
    right_gain = lax.dynamic_slice_in_dim(right_strength, first_state, state_count)
    regrouped = lax.all_to_all(density, "sys", split_axis=3, concat_axis=1, tiled=True)
    flattened = regrouped.reshape(2, regrouped.shape[1], -1)
    real_part = jnp.dot(herm_real, flattened[0], preferred_element_type=jnp.float32) - jnp.dot(
        herm_imag, flattened[1], preferred_element_type=jnp.float32
    )
    imag_part = jnp.dot(herm_real, flattened[1], preferred_element_type=jnp.float32) + jnp.dot(
        herm_imag, flattened[0], preferred_element_type=jnp.float32
    )
    product = jnp.stack([real_part, imag_part]).astype(jnp.bfloat16).reshape(regrouped.shape)
    system_rows = lax.all_to_all(product, "sys", split_axis=1, concat_axis=3, tiled=True)
    rc_count = lax.axis_size("rc")
    col_groups = rc_count // math.gcd(state_count, rc_count)
    per_device = state_count * col_groups // rc_count
    group_width = column_total // col_groups
    combined = jnp.moveaxis(
        density.reshape(2, state_count, pair_count, col_groups, group_width), 3, 2
    )
    combined = combined.reshape(2, state_count * col_groups, pair_count, group_width)
    combo_index = lax.axis_index("rc") * per_device + jnp.arange(per_device, dtype=jnp.int32)
    state_pick = (
        (combo_index // col_groups)[:, None] == jnp.arange(state_count, dtype=jnp.int32)[None, :]
    ).astype(jnp.float32)
    combo_left = jnp.sum(state_pick * left_gain[None, :], axis=1)
    combo_right = jnp.sum(state_pick * right_gain[None, :], axis=1)
    summed = ladder_local(
        lax.all_to_all(combined, "rc", split_axis=1, concat_axis=2, tiled=True),
        left_ops,
        right_ops,
        combo_left,
        combo_right,
        levels,
    )
    returned = lax.all_to_all(summed, "rc", split_axis=2, concat_axis=1, tiled=True)
    returned = returned.reshape(2, state_count, col_groups, pair_count, group_width)
    ladder_rows = jnp.moveaxis(returned, 2, 3).reshape(2, state_count, pair_count, column_total)
    pair_index = lax.axis_index("rc") * pair_count + jnp.arange(pair_count, dtype=jnp.int32)
    level_index = jnp.arange(levels, dtype=jnp.int32)
    left_pick = (pair_index[:, None] // levels == level_index[None, :]).astype(jnp.float32)
    right_pick = (pair_index[:, None] % levels == level_index[None, :]).astype(jnp.float32)
    damping = 0.5 * (
        jnp.sum(left_pick * left_damping[None, :], axis=1)
        + jnp.sum(right_pick * right_damping[None, :], axis=1)
    )
    system_term = system_rows.astype(jnp.float32)
    ladder = ladder_rows.astype(jnp.float32)
    real_in = density[0].astype(jnp.float32)
    imag_in = density[1].astype(jnp.float32)
    energy_grid = energies[None, None, :]
    damp_grid = damping[None, :, None]
    new_real = system_term[1] + ladder[1] - energy_grid * imag_in - damp_grid * real_in
    new_imag = -system_term[0] - ladder[0] + energy_grid * real_in - damp_grid * imag_in
    return jnp.stack([new_real, new_imag]).astype(jnp.bfloat16)


def solution(mesh):
    placed = (P(None, "sys", "rc", None), P(), P(), P(), P(), P(), P(), P(), P(), P(), P(), P())
    return jax.shard_map(
        shards, mesh=mesh, in_specs=placed, out_specs=P(None, "sys", "rc", None), check_vma=False
    )
```

profile of v0, /device:TPU:15, one launch (start us, length us, event | category | flops | bytes accessed | tf_op | source)
XLA Modules:
  0.0 636.5 jit_solution(9454477247624966088)
XLA Ops:
  0.0 16.1 %copy.126 = bf16[2,32,100,512]{2,1,0,3:T(8,128)(2,1)} copy(bf16[2,32,100,512]{3,1,2,0:T(8,128)(2,1)} %param.12) | data formatting | bytes 13107200 | tf_op args[0]
  23.2 9.4 %copy.133 = bf16[2,32,100,512]{3,2,0,1:T(8,128)(2,1)} copy(bf16[2,32,100,512]{3,1,2,0:T(8,128)(2,1)} %param.12) | data formatting | bytes 13107200 | tf_op args[0]
  32.7 81.2 %all-to-all-done = bf16[2,32,100,512]{2,1,0,3:T(8,128)(2,1)} async-done(((bf16[2,32,100,512]{2,1,0,3:T(8,128)(2,1)}), bf16[2,32,100,512]{2,1,0,3:T(8,128)(2,1)}, u32[]{:S(2)}, u32[]{:S(2)}) %all-to-all-start) | async-done | bytes 6553632 | tf_op jit(solution)/shard_map/all_to_all | solution.py:58
  122.3 14.7 %copy.127 = bf16[2,32,100,2,256]{4,2,1,3,0:T(8,128)(2,1)} copy(bf16[2,32,100,2,256]{2,1,0,4,3:T(8,128)(2,1)} %bitcast.1) | data formatting | bytes 13107200 | tf_op jit(solution)/shard_map/all_to_all | solution.py:58
  171.2 98.6 %all-to-all-done.2 = bf16[2,32,100,512]{3,2,0,1:T(8,128)(2,1)} async-done(((bf16[2,32,100,512]{3,2,0,1:T(8,128)(2,1)}), bf16[2,32,100,512]{3,2,0,1:T(8,128)(2,1)}, u32[]{:S(2)}, u32[]{:S(2)}) %all-to-all-start.2) | async-done | bytes 6553632 | tf_op jit(solution)/shard_map/all_to_all | solution.py:83
  269.8 8.0 %all-to-all-start.1 = ((bf16[2,64,100,256]{3,0,2,1:T(2,128)(2,1)}), bf16[2,64,100,256]{3,0,2,1:T(2,128)(2,1)}, u32[]{:S(2)}, u32[]{:S(2)}) async-start(bf16[2,64,100,256]{3,0,2,1:T(2,128)(2,1)} %copy.129), calls=%async_computation.1 | async-start | bytes 13107200 | tf_op jit(solution)/shard_map/all_to_all | solution.py:67
  284.2 10.3 %reshape.87 = bf16[2,2,40,20480]{3,2,1,0:T(8,128)(2,1)} reshape(bf16[2,2,16,100,512]{4,3,2,1,0:T(8,128)(2,1)} %bitcast.92) | data formatting | bytes 13107200 | tf_op jit(solution)/shard_map/reshape | solution.py:16
  294.4 9.5 %reshape.89 = bf16[2,2,40,40,512]{4,3,2,1,0:T(8,128)(2,1)} reshape(bf16[2,2,16,100,512]{4,3,2,1,0:T(8,128)(2,1)} %bitcast.93) | data formatting | bytes 13107200 | tf_op jit(solution)/shard_map/reshape | solution.py:19
  303.9 15.2 %convolution_bitcast_fusion = f32[2,2,80,20480]{3,2,1,0:T(8,128)} fusion(bf16[2,2,40,20480]{3,2,1,0:T(8,128)(2,1)} %reshape.87, bf16[40,40]{0,1:T(8,128)(2,1)S(1)} %get-tuple-element.15, bf16[40,40]{0,1:T(8,128)(2,1)S(1)} %get-tuple-element.16), kind=kOutput, calls=%fused_computation.4 | convolution fusion | flops 524300800 | bytes 32774400 | tf_op jit(solution)/shard_map/xa,ksam->ksxm/dot_general | solution.py:17
  319.1 14.4 %fusion.3 = f32[2,2,40,20480]{3,2,1,0:T(8,128)} fusion(f32[2,2,80,20480]{3,2,1,0:T(8,128)} %convolution_bitcast_fusion, f32[2]{0:T(128)S(1)} %get-tuple-element.6), kind=kLoop, calls=%fused_computation.8 | loop fusion | flops 6553600 | bytes 39321608 | tf_op jit(solution)/shard_map/add | solution.py:18
  333.5 13.2 %reshape.88 = f32[2,2,1600,512]{3,2,1,0:T(8,128)} reshape(f32[2,2,40,20480]{3,2,1,0:T(8,128)} %fusion.3) | data formatting | bytes 26214400 | tf_op jit(solution)/shard_map/reshape | solution.py:27
  346.7 15.3 %convolution_bitcast_fusion.1 = f32[2,2,40,80,512]{4,3,2,1,0:T(8,128)} fusion(bf16[2,2,40,40,512]{4,3,2,1,0:T(8,128)(2,1)} %reshape.89, bf16[40,40]{0,1:T(8,128)(2,1)S(1)} %get-tuple-element.17, bf16[40,40]{0,1:T(8,128)(2,1)S(1)} %get-tuple-element.18), kind=kOutput, calls=%fused_computation.12 | convolution fusion | flops 524300800 | bytes 32774400 | tf_op jit(solution)/shard_map/yb,ksabc->ksayc/dot_general | solution.py:20
  362.1 10.7 %fusion.2 = f32[2,2,40,40,512]{4,3,2,1,0:T(8,128)S(1)} fusion(f32[2,2,40,80,512]{4,3,2,1,0:T(8,128)} %convolution_bitcast_fusion.1, f32[2]{0:T(128)S(1)} %get-tuple-element.5), kind=kLoop, calls=%fused_computation.6 | loop fusion | flops 6553600 | bytes 39321608 | tf_op jit(solution)/shard_map/add | solution.py:24
  377.5 48.1 %copy.137 = bf16[2,2,1600,512]{3,1,0,2:T(2,128)(2,1)} copy(bf16[2,2,1600,512]{3,2,1,0:T(8,128)(2,1)} %fusion.4) | data formatting | bytes 13107200 | tf_op jit(solution)/shard_map/convert_element_type | solution.py:30
  431.2 12.7 %copy.156 = f32[2,2,32,100,256]{4,1,2,3,0:T(2,128)S(1)} copy(bf16[2,2,32,100,256]{4,0,3,2,1:T(2,128)(2,1)} %bitcast.22) | data formatting | bytes 19660800 | tf_op jit(solution)/shard_map/convert_element_type | solution.py:101
  443.9 8.5 %fusion.37 = (f32[1,32,100,2,256]{4,3,1,2,0:T(2,128)}, f32[1,32,100,2,256]{4,3,1,2,0:T(2,128)}) fusion(f32[2,32,100,2,256]{4,3,1,2,0:T(2,128)S(1)} %bitcast.97), kind=kLoop, calls=%fused_computation.72 | loop fusion | flops 1638400 | bytes 26214400 | tf_op jit(solution)/shard_map/slice | solution.py:107
  452.4 9.2 %neg.8 = f32[1,32,100,512]{3,1,2,0:T(8,128)} reshape(f32[1,32,100,2,256]{4,3,1,2,0:T(2,128)} %get-tuple-element.10) | data formatting | bytes 13107200 | tf_op jit(solution)/shard_map/neg | solution.py:108
  461.6 9.1 %slice.53 = f32[1,32,100,512]{3,1,2,0:T(8,128)} reshape(f32[1,32,100,2,256]{4,3,1,2,0:T(2,128)} %get-tuple-element.9) | data formatting | bytes 13107200 | tf_op jit(solution)/shard_map/slice | solution.py:107
  470.7 103.3 %all-to-all-done.3 = bf16[2,2,1600,512]{3,1,0,2:T(2,128)(2,1)} async-done(((bf16[2,2,1600,512]{3,1,0,2:T(2,128)(2,1)}), bf16[2,2,1600,512]{3,1,0,2:T(2,128)(2,1)}, u32[]{:S(2)}, u32[]{:S(2)}) %all-to-all-start.3) | async-done | bytes 6553632 | tf_op jit(solution)/shard_map/all_to_all | solution.py:90
  574.0 9.7 %copy_convert_fusion = f32[2,2,1600,512]{3,2,1,0:T(8,128)} fusion(bf16[2,2,1600,512]{3,1,0,2:T(2,128)(2,1)} %all-to-all-done.3), kind=kLoop, calls=%fused_computation.29 | loop fusion | flops 3276800 | bytes 19660800 | tf_op jit(solution)/shard_map/convert_element_type | solution.py:102
  583.7 13.8 %reshape.92 = f32[2,2,16,100,512]{4,3,2,1,0:T(8,128)} reshape(f32[2,2,1600,512]{3,2,1,0:T(8,128)} %copy_convert_fusion) | data formatting | bytes 26214400 | tf_op jit(solution)/shard_map/convert_element_type | solution.py:102
  597.5 11.7 %fusion.36 = (f32[1,16,2,100,512]{4,3,1,2,0:T(8,128)}, f32[1,16,2,100,512]{4,3,1,2,0:T(8,128)}) fusion(f32[2,16,2,100,512]{4,3,1,2,0:T(8,128)} %bitcast.96), kind=kLoop, calls=%fused_computation.71 | loop fusion | bytes 26214400 | tf_op jit(solution)/shard_map/slice | solution.py:107
  609.3 7.5 %copy.139 = f32[1,16,2,100,512]{4,3,2,1,0:T(8,128)} copy(f32[1,16,2,100,512]{4,3,1,2,0:T(8,128)} %get-tuple-element.7) | data formatting | bytes 13107200 | tf_op jit(solution)/shard_map/slice | solution.py:107
  620.5 15.8 %fusion.7 = (bf16[2,32,100,512]{3,1,2,0:T(8,128)(2,1)}, bf16[2,32,100,512]{3,1,2,0:T(8,128)(2,1)}) fusion(f32[1,32,100,512]{3,1,2,0:T(8,128)} %slice.53, f32[1,32,100,512]{3,2,1,0:T(8,128)} %bitcast.104, f32[100]{0:T(128)S(1)} %add_multiply_fusion, f32[512]{0:T(512)S(1)} %copy-done.9, ...), kind=kLoop, output_to_operand_aliasing={{0}: (7, {}), {1}: (7, {})}, calls=%fused_computation.21 | loop fusion | flops 22937600 | bytes 39848336 | tf_op jit(solution)/shard_map/convert.4
  (78 shorter events, 70.1 us)
Async XLA Ops:
  16.1 97.8 %all-to-all-start = ((bf16[2,32,100,512]{2,1,0,3:T(8,128)(2,1)}), bf16[2,32,100,512]{2,1,0,3:T(8,128)(2,1)}, u32[]{:S(2)}, u32[]{:S(2)}) async-start(bf16[2,32,100,512]{2,1,0,3:T(8,128)(2,1)} %copy.126), calls=%async_computation | async-start | bytes 16777216 | tf_op jit(solution)/shard_map/all_to_all | solution.py:58
  32.6 88.7 %copy-start.10 = (f32[64]{0:T(128)S(1)}, f32[64]{0:T(128)}, u32[]{:S(2)}) copy-start(f32[64]{0:T(128)} %param.19) | copy-start | bytes 772
  32.6 88.8 %copy-start.11 = (f32[64]{0:T(128)S(1)}, f32[64]{0:T(128)}, u32[]{:S(2)}) copy-start(f32[64]{0:T(128)} %param.20) | copy-start | bytes 772
  32.6 88.8 %copy-start.5 = (bf16[40,40]{1,0:T(8,128)(2,1)S(1)}, bf16[40,40]{1,0:T(8,128)(2,1)}, u32[]{:S(2)}) copy-start(bf16[40,40]{1,0:T(8,128)(2,1)} %param.15) | copy-start | bytes 9604
  32.6 88.9 %copy-start.4 = (bf16[40,40]{1,0:T(8,128)(2,1)S(1)}, bf16[40,40]{1,0:T(8,128)(2,1)}, u32[]{:S(2)}) copy-start(bf16[40,40]{1,0:T(8,128)(2,1)} %param.16) | copy-start | bytes 9604
  32.6 89.0 %copy-start.7 = (bf16[40,40]{1,0:T(8,128)(2,1)S(1)}, bf16[40,40]{1,0:T(8,128)(2,1)}, u32[]{:S(2)}) copy-start(bf16[40,40]{1,0:T(8,128)(2,1)} %param.17) | copy-start | bytes 9604
  32.6 89.1 %copy-start.6 = (bf16[40,40]{1,0:T(8,128)(2,1)S(1)}, bf16[40,40]{1,0:T(8,128)(2,1)}, u32[]{:S(2)}) copy-start(bf16[40,40]{1,0:T(8,128)(2,1)} %param.18) | copy-start | bytes 9604
  32.6 89.1 %copy-start.8 = (bf16[64,64]{1,0:T(8,128)(2,1)S(1)}, bf16[64,64]{1,0:T(8,128)(2,1)}, u32[]{:S(2)}) copy-start(bf16[64,64]{1,0:T(8,128)(2,1)} %param.13) | copy-start | bytes 24580
  32.6 89.3 %copy-start.3 = (bf16[64,64]{1,0:T(8,128)(2,1)S(1)}, bf16[64,64]{1,0:T(8,128)(2,1)}, u32[]{:S(2)}) copy-start(bf16[64,64]{1,0:T(8,128)(2,1)} %param.14) | copy-start | bytes 24580
  113.8 155.9 %all-to-all-start.2 = ((bf16[2,32,100,512]{3,2,0,1:T(8,128)(2,1)}), bf16[2,32,100,512]{3,2,0,1:T(8,128)(2,1)}, u32[]{:S(2)}, u32[]{:S(2)}) async-start(bf16[2,32,100,512]{3,2,0,1:T(8,128)(2,1)} %copy.133), calls=%async_computation.2 | async-start | bytes 13631488 | tf_op jit(solution)/shard_map/all_to_all | solution.py:83
  141.8 1.7 copy-start
  157.0 5.2 copy-start.2
  269.8 155.9 %all-to-all-start.1 = ((bf16[2,64,100,256]{3,0,2,1:T(2,128)(2,1)}), bf16[2,64,100,256]{3,0,2,1:T(2,128)(2,1)}, u32[]{:S(2)}, u32[]{:S(2)}) async-start(bf16[2,64,100,256]{3,0,2,1:T(2,128)(2,1)} %copy.129), calls=%async_computation.1 | async-start | bytes 13107200 | tf_op jit(solution)/shard_map/all_to_all | solution.py:67
  346.7 26.0 %slice-start.2 = ((s8[13107200]{0:T(1024)(128)(4,1)}), s8[524288]{0:T(1024)(128)(4,1)S(1)}, s32[]{:S(2)}) async-start(s8[13107200]{0:T(1024)(128)(4,1)} %bitcast.98), calls=%async_computation.6 | async-start | bytes 1048576
  346.7 26.0 %slice-start.3 = ((s8[13107200]{0:T(1024)(128)(4,1)}), s8[4194304]{0:T(1024)(128)(4,1)S(1)}, s32[]{:S(2)}) async-start(s8[13107200]{0:T(1024)(128)(4,1)} %bitcast.98), calls=%async_computation.7 | async-start | bytes 8388608
  362.1 10.7 %slice-start.4 = ((s8[13107200]{0:T(1024)(128)(4,1)}), s8[4194304]{0:T(1024)(128)(4,1)S(1)}, s32[]{:S(2)}) async-start(s8[13107200]{0:T(1024)(128)(4,1)} %bitcast.98), calls=%async_computation.8 | async-start | bytes 8388608
  362.1 11.0 %slice-start.5 = ((s8[13107200]{0:T(1024)(128)(4,1)}), s8[4194304]{0:T(1024)(128)(4,1)S(1)}, s32[]{:S(2)}) async-start(s8[13107200]{0:T(1024)(128)(4,1)} %bitcast.98), calls=%async_computation.9 | async-start | bytes 8388608
  425.6 5.3 copy-start.12
  425.6 5.4 copy-start.13
  425.6 148.3 %all-to-all-start.3 = ((bf16[2,2,1600,512]{3,1,0,2:T(2,128)(2,1)}), bf16[2,2,1600,512]{3,1,0,2:T(2,128)(2,1)}, u32[]{:S(2)}, u32[]{:S(2)}) async-start(bf16[2,2,1600,512]{3,1,0,2:T(2,128)(2,1)} %copy.137), calls=%async_computation.3 | async-start | bytes 13107200 | tf_op jit(solution)/shard_map/all_to_all | solution.py:90
  609.3 7.5 %copy-start.1 = (f32[1,16,2,100,512]{4,3,1,2,0:T(8,128)S(1)}, f32[1,16,2,100,512]{4,3,1,2,0:T(8,128)}, u32[]{:S(2)}) copy-start(f32[1,16,2,100,512]{4,3,1,2,0:T(8,128)} %get-tuple-element.8) | copy-start | bytes 19660804
  609.3 11.2 %slice-start = ((s8[6553600]{0:T(1024)(128)(4,1)}), s8[4194304]{0:T(1024)(128)(4,1)S(1)}, s32[]{:S(2)}) async-start(s8[6553600]{0:T(1024)(128)(4,1)} %bitcast.94), calls=%async_computation.4 | async-start | bytes 8388608
  616.8 3.7 slice-start.1
  616.8 3.7 copy-start.9
where the time goes:
time: 644 us; the launch traced here: 636 us
  waiting for transfers between devices  283 us (44%)
  local copies, waits for them, and re-layouts  219 us (34%)
  other arithmetic  66.6 us (10%)
  matrix products  40 us (6%)
  starting transfers between devices  27.9 us (4%)
    all_to_all x1, waiting for transfers between devices, shards(): lax.all_to_all(summed, 'rc', split_axis=2, concat_axis=1, tiled=True)  103 us
    all_to_all x1, waiting for transfers between devices, shards(): lax.all_to_all(combined, 'rc', split_axis=1, concat_axis=2, tiled=True)  98.6 us
    all_to_all x1, waiting for transfers between devices, shards(): lax.all_to_all(density, 'sys', split_axis=3, concat_axis=1, tiled=True)  81.2 us
    convert_element_type x1, local copies, waits for them, and re-layouts, ladder_local(): return summed.astype(jnp.bfloat16)  48.1 us
    unnamed x45, local copies, waits for them, and re-layouts  28 us
    slice x2, local copies, waits for them, and re-layouts, shards(): ladder[1]  19.2 us
    another operation x3, local copies, waits for them, and re-layouts, shards(): jnp.stack([real_part, imag_part]).astype(jnp.bfloat16)  16.5 us
    another operation x2, other arithmetic  15.8 us
  transfers between devices with their start and end apart: 4, of which 3 were waited for; matrix products, arithmetic and copies ran while one was open for 39% of the time, Pallas kernels for 0%

commit v1 on v0

--- a/solution.py
+++ b/solution.py
@@ -1,9 +1,16 @@
+import functools
 import math
 
 import jax
 import jax.numpy as jnp
 from jax import lax
+from jax.experimental import pallas as pl
+from jax.experimental.pallas import tpu as pltpu
 from jax.sharding import PartitionSpec as P
+
+ROWS = 16
+LANES = 128
+STEP = 5
 
 
 def symmetric(matrix, factor):
@@ -109,8 +116,414 @@
     return jnp.stack([new_real, new_imag]).astype(jnp.bfloat16)
 
 
+def one_hot(shape, hit):
+    row = lax.broadcasted_iota(jnp.int32, shape, 0)
+    col = lax.broadcasted_iota(jnp.int32, shape, 1)
+    return jnp.where(hit(row, col), 1.0, 0.0).astype(jnp.bfloat16)
+
+
+def product(left, right):
+    return jnp.dot(left, right, preferred_element_type=jnp.float32)
+
+
+def picked(left, right):
+    return product(left, right).astype(jnp.bfloat16)
+
+
+def symmetric_tile(matrix, factor):
+    size = matrix.shape[0]
+    eye = one_hot((size, size), lambda row, col: row == col)
+    turned = lax.dot_general(
+        matrix, eye, (((0,), (0,)), ((), ())), preferred_element_type=jnp.float32
+    )
+    return ((matrix.astype(jnp.float32) + factor * turned) * 0.5).astype(jnp.bfloat16)
+
+
+def ladder_matrix(ham, coupling, strength, first_state):
+    levels = ham.shape[0]
+    size = levels * ROWS
+    tall = one_hot((size, levels), lambda row, col: row // ROWS == col)
+    wide = one_hot((levels, size), lambda row, col: row == col // ROWS)
+    ham_all = product(picked(tall, symmetric_tile(ham, 1.0)), wide)
+    coupling_all = product(picked(tall, symmetric_tile(coupling, 1.0)), wide)
+    states = strength.shape[1]
+    row = lax.broadcasted_iota(jnp.int32, (size, states), 0)
+    col = lax.broadcasted_iota(jnp.int32, (size, states), 1)
+    gain = jnp.sum(
+        jnp.where(col == first_state + row % ROWS, strength, 0.0), axis=1, keepdims=True
+    )
+    row = lax.broadcasted_iota(jnp.int32, (size, size), 0)
+    col = lax.broadcasted_iota(jnp.int32, (size, size), 1)
+    mixed = ham_all + gain * coupling_all
+    return jnp.where(row % ROWS == col % ROWS, mixed, 0.0).astype(jnp.bfloat16)
+
+
+def system_matrix(system_real, system_imag, sys_index, local):
+    states = system_real.shape[0]
+    rows = one_hot((local, states), lambda row, col: col == row + local * sys_index)
+    real = picked(rows, symmetric_tile(system_real, 1.0))
+    imag = picked(rows, symmetric_tile(system_imag, -1.0))
+
+    def place(part):
+        def hit(row, col):
+            block = col // local
+            side = jnp.where(block < 2, sys_index, 1 - sys_index)
+            return (block % 2 == part) & (row == col % local + local * side)
+
+        return one_hot((states, 2 * states), hit)
+
+    to_real, to_imag = place(0), place(1)
+    upper = product(imag, to_real) + product(real, to_imag)
+    lower = product(imag, to_imag) - product(real, to_real)
+    return jnp.concatenate([upper, lower], axis=0).astype(jnp.bfloat16)
+
+
+def section_kernel(
+    count,
+    dens,
+    system_real,
+    system_imag,
+    left_ham,
+    left_coupling,
+    right_ham,
+    right_coupling,
+    left_strength,
+    right_strength,
+    left_damping,
+    right_damping,
+    energies,
+    rest_out,
+    left_out,
+    mine,
+    other,
+    level,
+    taken,
+    given,
+    rest,
+    left_mat,
+    right_mat,
+    sys_mat,
+    fwd_send,
+    fwd_recv,
+    ret_send,
+    ret_recv,
+    sys_send,
+    sys_recv,
+    level_sem,
+    mine_sem,
+    out_sem,
+):
+    me = lax.axis_index("rc")
+    sys_index = lax.axis_index("sys")
+    _, halves, half, local, columns = dens.shape
+    levels = 2 * half
+    row_blocks, lane_blocks = local // ROWS, columns // LANES
+    chunks = half // STEP
+    odd = lax.rem(me, 2)
+    partner = me + 1 - 2 * odd
+    shared = (halves - 1) * (1 - odd)
+
+    def task(rank):
+        part = rank // (row_blocks * lane_blocks)
+        row = lax.rem(rank // lane_blocks, row_blocks) * ROWS
+        lane = lax.rem(rank, lane_blocks) * LANES
+        return part, pl.ds(pl.multiple_of(row, ROWS), ROWS), pl.ds(pl.multiple_of(lane, LANES), LANES)
+
+    def peer(offset):
+        return lax.rem(me + offset, count)
+
+    def part_of(rank, chunk):
+        part, row, lane = task(rank)
+        return dens.at[part, :, pl.ds(chunk * STEP, STEP), row, lane]
+
+    def forward(chunk, rank, owner):
+        return pltpu.make_async_remote_copy(
+            src_ref=part_of(rank, chunk),
+            dst_ref=taken.at[chunk, pl.ds(owner * halves, halves)],
+            send_sem=fwd_send.at[chunk, rank],
+            recv_sem=fwd_recv.at[chunk, owner],
+            device_id={"rc": rank},
+            device_id_type=pl.DeviceIdType.MESH,
+        )
+
+    def forward_own(chunk):
+        return pltpu.make_async_copy(
+            part_of(me, chunk), taken.at[chunk, pl.ds(me * halves, halves)], fwd_recv.at[chunk, me]
+        )
+
+    def landing(rank, chunk):
+        part, row, lane = task(rank)
+        return left_out.at[1 - part, :, pl.ds(chunk * STEP, STEP), row, lane]
+
+    def giveback(chunk, rank, worker):
+        return pltpu.make_async_remote_copy(
+            src_ref=given.at[chunk, pl.ds(rank * halves, halves)],
+            dst_ref=landing(worker, chunk),
+            send_sem=ret_send.at[chunk, rank],
+            recv_sem=ret_recv.at[chunk, worker],
+            device_id={"rc": rank},
+            device_id_type=pl.DeviceIdType.MESH,
+        )
+
+    def giveback_own(chunk):
+        return pltpu.make_async_copy(
+            given.at[chunk, pl.ds(me * halves, halves)], landing(me, chunk), ret_recv.at[chunk, me]
+        )
+
+    def swap(index):
+        return pltpu.make_async_remote_copy(
+            src_ref=dens.at[:, index],
+            dst_ref=other.at[:, index],
+            send_sem=sys_send.at[index],
+            recv_sem=sys_recv.at[index],
+            device_id={"sys": 1 - sys_index},
+            device_id_type=pl.DeviceIdType.MESH,
+        )
+
+    barrier = pltpu.get_barrier_semaphore()
+
+    @pl.loop(1, count)
+    def _(offset):
+        pl.semaphore_signal(
+            barrier, inc=1, device_id={"rc": peer(offset)}, device_id_type=pl.DeviceIdType.MESH
+        )
+
+    pl.semaphore_signal(
+        barrier, inc=1, device_id={"sys": 1 - sys_index}, device_id_type=pl.DeviceIdType.MESH
+    )
+    pl.semaphore_wait(barrier, count)
+
+    level_copy = pltpu.make_async_remote_copy(
+        src_ref=dens.at[:, shared],
+        dst_ref=level.at[:, odd],
+        send_sem=level_sem.at[0],
+        recv_sem=level_sem.at[1],
+        device_id={"rc": partner},
+        device_id_type=pl.DeviceIdType.MESH,
+    )
+    level_copy.start()
+    level_own = pltpu.make_async_copy(dens.at[:, shared], level.at[:, odd], level_sem.at[2])
+    level_own.start()
+    mine_copy = pltpu.make_async_copy(dens, mine, mine_sem)
+    mine_copy.start()
+
+    @pl.loop(0, chunks)
+    def _(chunk):
+        forward_own(chunk).start()
+
+        @pl.loop(1, count)
+        def _(offset):
+            forward(chunk, peer(offset), me).start()
+
+    @pl.loop(0, halves)
+    def _(index):
+        swap(index).start()
+
+    my_part = me // (row_blocks * lane_blocks)
+    my_row = lax.rem(me // lane_blocks, row_blocks) * ROWS
+    left_mat[...] = ladder_matrix(
+        left_ham[...], left_coupling[...], left_strength[...], sys_index * local + my_row
+    )
+    for block in range(row_blocks):
+        right_mat[block] = ladder_matrix(
+            right_ham[...],
+            right_coupling[...],
+            right_strength[...],
+            sys_index * local + block * ROWS,
+        )
+    sys_mat[...] = system_matrix(system_real[...], system_imag[...], sys_index, local)
+
+    mine_copy.wait()
+    level_own.wait()
+    level_copy.wait()
+    full_levels = halves // 2
+
+    @pl.loop(0, 2)
+    def _(part):
+        sign = jnp.where(part == 1, 1.0, -1.0)
+        for block in range(row_blocks):
+            row = pl.ds(block * ROWS, ROWS)
+
+            @pl.loop(0, full_levels)
+            def _(number):
+                first = odd + 2 * number
+                held = mine[part, pl.ds(first, 2), :, row, :].reshape(levels * ROWS, columns)
+                term = product(right_mat[block], held) * sign
+                rest[1 - part, pl.ds(first, 2), :, row, :] = term.reshape(2, half, ROWS, columns)
+
+            held = level[part, :, :, row, :].reshape(levels * ROWS, columns)
+            rows = pl.ds(pl.multiple_of(odd * half * ROWS, half * ROWS), half * ROWS)
+            term = product(right_mat[block, rows, :], held) * sign
+            rest[1 - part, shared, :, row, :] = term.reshape(half, ROWS, columns)
+
+    my_sign = jnp.where(my_part == 1, 1.0, -1.0)
+
+    @pl.loop(0, chunks)
+    def _(chunk):
+        forward_own(chunk).wait()
+
+        @pl.loop(1, count)
+        def _(offset):
+            forward(chunk, me, peer(offset)).wait_recv()
+
+        for side in range(2):
+            held = jnp.concatenate(
+                [
+                    jnp.concatenate(
+                        [taken[chunk, 2 * number + side, at] for number in range(levels)], axis=0
+                    )
+                    for at in range(STEP)
+                ],
+                axis=1,
+            )
+            term = (product(left_mat[...], held) * my_sign).astype(jnp.bfloat16)
+            for at in range(STEP):
+                for number in range(levels):
+                    given[chunk, 2 * number + side, at] = term[
+                        number * ROWS : (number + 1) * ROWS, at * LANES : (at + 1) * LANES
+                    ]
+        giveback_own(chunk).start()
+
+        @pl.loop(1, count)
+        def _(offset):
+            giveback(chunk, peer(offset), me).start()
+
+    @pl.loop(0, halves)
+    def _(index):
+        swap(index).wait_recv()
+
+        @pl.loop(0, half)
+        def _(at):
+            pair = (me * halves + index) * half + at
+            damping = 0.5 * (left_damping[pair // levels] + right_damping[lax.rem(pair, levels)])
+            real, imag = mine[0, index, at], mine[1, index, at]
+            held = jnp.concatenate([real, imag, other[0, index, at], other[1, index, at]], axis=0)
+            term = product(sys_mat[...], held)
+            real, imag = real.astype(jnp.float32), imag.astype(jnp.float32)
+            energy = energies[...]
+            new_real = term[:local] + rest[0, index, at] - energy * imag - damping * real
+            new_imag = term[local:] + rest[1, index, at] + energy * real - damping * imag
+            other[0, index, at] = new_real.astype(jnp.bfloat16)
+            other[1, index, at] = new_imag.astype(jnp.bfloat16)
+
+        pltpu.make_async_copy(other.at[:, index], rest_out.at[:, index], out_sem.at[index]).start()
+
+    @pl.loop(0, halves)
+    def _(index):
+        swap(index).wait_send()
+        pltpu.make_async_copy(other.at[:, index], rest_out.at[:, index], out_sem.at[index]).wait()
+
+    @pl.loop(0, chunks)
+    def _(chunk):
+        giveback_own(chunk).wait()
+
+        @pl.loop(1, count)
+        def _(offset):
+            rank = peer(offset)
+            forward(chunk, rank, me).wait_send()
+            giveback(chunk, rank, me).wait_send()
+            giveback(chunk, me, rank).wait_recv()
+
+
+def exchanged(
+    density,
+    system_real,
+    system_imag,
+    left_ham,
+    left_coupling,
+    right_ham,
+    right_coupling,
+    left_strength,
+    right_strength,
+    left_damping,
+    right_damping,
+    energies,
+):
+    count = lax.axis_size("rc")
+    levels = left_ham.shape[0]
+    half = levels // 2
+    _, local, pairs, columns = density.shape
+    halves = pairs // half
+    chunks = half // STEP
+    size = levels * ROWS
+    row_blocks = local // ROWS
+    dens = jnp.transpose(density, (0, 2, 1, 3)).reshape(2, halves, half, local, columns)
+    whole = pl.BlockSpec(memory_space=pltpu.VMEM)
+    scalars = pl.BlockSpec(memory_space=pltpu.SMEM)
+    anywhere = pl.BlockSpec(memory_space=pl.ANY)
+    slab = jax.ShapeDtypeStruct(dens.shape, jnp.bfloat16)
+    rest, left = pl.pallas_call(
+        functools.partial(section_kernel, count),
+        out_shape=[slab, slab],
+        in_specs=[anywhere] + [whole] * 8 + [scalars] * 2 + [whole],
+        out_specs=[anywhere, anywhere],
+        scratch_shapes=[
+            pltpu.VMEM(dens.shape, jnp.bfloat16),
+            pltpu.VMEM(dens.shape, jnp.bfloat16),
+            pltpu.VMEM((2, 2, half, local, columns), jnp.bfloat16),
+            pltpu.VMEM((chunks, count * halves, STEP, ROWS, LANES), jnp.bfloat16),
+            pltpu.VMEM((chunks, count * halves, STEP, ROWS, LANES), jnp.bfloat16),
+            pltpu.VMEM(dens.shape, jnp.float32),
+            pltpu.VMEM((size, size), jnp.bfloat16),
+            pltpu.VMEM((row_blocks, size, size), jnp.bfloat16),
+            pltpu.VMEM((2 * local, 4 * local), jnp.bfloat16),
+            pltpu.SemaphoreType.DMA((chunks, count)),
+            pltpu.SemaphoreType.DMA((chunks, count)),
+            pltpu.SemaphoreType.DMA((chunks, count)),
+            pltpu.SemaphoreType.DMA((chunks, count)),
+            pltpu.SemaphoreType.DMA((halves,)),
+            pltpu.SemaphoreType.DMA((halves,)),
+            pltpu.SemaphoreType.DMA((3,)),
+            pltpu.SemaphoreType.DMA,
+            pltpu.SemaphoreType.DMA((halves,)),
+        ],
+        compiler_params=pltpu.CompilerParams(
+            collective_id=0, has_side_effects=True, vmem_limit_bytes=60 * 2**20
+        ),
+        cost_estimate=pl.CostEstimate(
+            flops=10 * 10**9, bytes_accessed=5 * dens.size * 2, transcendentals=0
+        ),
+    )(
+        dens,
+        system_real,
+        system_imag,
+        left_ham,
+        left_coupling,
+        right_ham,
+        right_coupling,
+        left_strength[None, :],
+        right_strength[None, :],
+        left_damping,
+        right_damping,
+        energies[None, :],
+    )
+    total = (rest.astype(jnp.float32) + left.astype(jnp.float32)).astype(jnp.bfloat16)
+    return jnp.transpose(total.reshape(2, pairs, local, columns), (0, 2, 1, 3))
+
+
+def fits(mesh, shapes):
+    count, sides = mesh.shape["rc"], mesh.shape["sys"]
+    _, states, pairs, columns = shapes[0]
+    levels = shapes[3][0]
+    if sides != 2 or levels % 2 or pairs % count or states % (2 * ROWS) or columns % LANES:
+        return False
+    half, local_pairs = levels // 2, pairs // count
+    tasks = 2 * (states // (2 * ROWS)) * (columns // LANES)
+    return (
+        tasks == count
+        and half % STEP == 0
+        and local_pairs % half == 0
+        and local_pairs // half % 2 == 1
+    )
+
+
 def solution(mesh):
     placed = (P(None, "sys", "rc", None), P(), P(), P(), P(), P(), P(), P(), P(), P(), P(), P())
-    return jax.shard_map(
-        shards, mesh=mesh, in_specs=placed, out_specs=P(None, "sys", "rc", None), check_vma=False
-    )
+
+    def run(*arrays):
+        body = exchanged if fits(mesh, [array.shape for array in arrays]) else shards
+        return jax.shard_map(
+            body, mesh=mesh, in_specs=placed, out_specs=P(None, "sys", "rc", None), check_vma=False
+        )(*arrays)
+
+    return run

time: 644 us -> 304 us (0.47)
  Pallas kernels: 0 us -> 291 us
  waiting for transfers between devices: 283 us -> 0 us
  local copies, waits for them, and re-layouts: 219 us -> 0 us
  other arithmetic: 66.6 us -> 11.4 us
  matrix products: 40 us -> 0 us
  starting transfers between devices: 27.9 us -> 0 us
    pallas_call x0 -> x1, Pallas kernels: none -> 291 us  [exchanged(): pl.pallas_call(functools.partial(section_kernel, count), out_shape=[slab,...]
    all_to_all x4 -> x0, waiting for transfers between devices: 283 us -> none  [the longest x1 103 us: shards(): lax.all_to_all(summed, 'rc', split_axis=2, concat_axis=1, tiled=True)]
    convert_element_type x9 -> x0, local copies, waits for them, and re-layouts: 75.2 us -> none  [the longest x1 48.1 us: ladder_local(): return summed.astype(jnp.bfloat16)]
    dot_general x6 -> x0, matrix products: 40 us -> none  [the longest x1 15.3 us: ladder_local(): jnp.einsum('yb,ksabc->ksayc', right_ops, deepened, preferred_element_type...]
    slice x5 -> x0, local copies, waits for them, and re-layouts: 35.5 us -> none  [the longest x2 19.2 us: shards(): ladder[1]]
    reshape x3 -> x0, local copies, waits for them, and re-layouts: 32.9 us -> none  [the longest x1 13.2 us: ladder_local(): left_term.reshape(item_count, group_count, all_pairs, column_count)]
    unnamed x45 -> x0, local copies, waits for them, and re-layouts: 28 us -> none
    all_to_all x4 -> x0, starting transfers between devices: 27.9 us -> none  [the longest x1 7.99 us: shards(): lax.all_to_all(product, 'sys', split_axis=1, concat_axis=3, tiled=True)]
  transfers between devices with their start and end apart: 4 -> 0, of which waited for: 3 -> 0; matrix products, arithmetic and copies ran while one was open for 39% -> 0% of each run, Pallas kernels for 0% -> 0%
where the time goes in v1:
time: 304 us; the launch traced here: 303 us
  Pallas kernels  291 us (96%)
  other arithmetic  11.4 us (4%)
    pallas_call x1, Pallas kernels, exchanged(): pl.pallas_call(functools.partial(section_kernel, count), out_shape=[slab,...  291 us
    convert_element_type x1, other arithmetic, exchanged(): (rest.astype(jnp.float32) + left.astype(jnp.float32)).astype(jnp.bfloat16)  11.4 us

profile of v1, /device:TPU:15, one launch (start us, length us, event | category | flops | bytes accessed | tf_op | source)
XLA Modules:
  0.0 302.7 jit_solution(2159084910652778552)
XLA Ops:
  0.0 291.4 %shard_map.118 = (bf16[2,5,20,32,512]{4,3,2,1,0:T(8,128)(2,1)}, bf16[2,5,20,32,512]{4,3,2,1,0:T(8,128)(2,1)}) custom-call(bf16[2,5,20,32,512]{4,3,2,1,0:T(8,128)(2,1)} %bitcast.9, bf16[64,64]{1,0:T(8,128)(2,1)} %system_real.1, bf16[64,64]{1,0:T(8,128)(2,1)} %system_imag.1, bf16[40,40]{1,0:T(8,128)(2,1)} %left_ham.1, bf16[40,40]{1,0:T(8,128)(2,1)} %left_coupling.1, ...), custom_call_target="tpu_custom_call" | custom-call | flops 10000000000 | bytes 32768000 | tf_op jit(solution)/shard_map/pallas_call | solution.py:455
  291.4 11.4 %add_convert_fusion = bf16[2,5,20,32,512]{4,3,2,1,0:T(8,128)(2,1)} fusion(bf16[2,5,20,32,512]{4,3,2,1,0:T(8,128)(2,1)} %get-tuple-element.8, bf16[2,5,20,32,512]{4,3,2,1,0:T(8,128)(2,1)} %get-tuple-element.7), kind=kLoop, calls=%fused_computation | loop fusion | flops 13107200 | bytes 19660800 | tf_op jit(solution)/shard_map/convert_element_type | solution.py:500

commit v2 on v1

--- a/solution.py
+++ b/solution.py
@@ -229,8 +229,10 @@
         lane = lax.rem(rank, lane_blocks) * LANES
         return part, pl.ds(pl.multiple_of(row, ROWS), ROWS), pl.ds(pl.multiple_of(lane, LANES), LANES)
 
-    def peer(offset):
-        return lax.rem(me + offset, count)
+    def peer(turn):
+        side = count // 2
+        other_side = lax.rem(turn, 2)
+        return lax.rem(me // side + other_side, 2) * side + lax.rem(me + turn // 2, side)
 
     def part_of(rank, chunk):
         part, row, lane = task(rank)
@@ -315,7 +317,9 @@
         def _(offset):
             forward(chunk, peer(offset), me).start()
 
-    @pl.loop(0, halves)
+        swap(chunk).start()
+
+    @pl.loop(chunks, halves)
     def _(index):
         swap(index).start()
 
@@ -423,6 +427,10 @@
             forward(chunk, rank, me).wait_send()
             giveback(chunk, rank, me).wait_send()
             giveback(chunk, me, rank).wait_recv()
+
+
+def add_kernel(rest, left, total):
+    total[...] = (rest[...].astype(jnp.float32) + left[...].astype(jnp.float32)).astype(jnp.bfloat16)
 
 
 def exchanged(
@@ -497,7 +505,17 @@
         right_damping,
         energies[None, :],
     )
-    total = (rest.astype(jnp.float32) + left.astype(jnp.float32)).astype(jnp.bfloat16)
+    block = pl.BlockSpec((1, 1, half, local, columns), lambda part, index: (part, index, 0, 0, 0))
+    total = pl.pallas_call(
+        add_kernel,
+        out_shape=slab,
+        grid=(2, halves),
+        in_specs=[block, block],
+        out_specs=block,
+        cost_estimate=pl.CostEstimate(
+            flops=dens.size, bytes_accessed=3 * dens.size * 2, transcendentals=0
+        ),
+    )(rest, left)
     return jnp.transpose(total.reshape(2, pairs, local, columns), (0, 2, 1, 3))
 
 
@@ -514,6 +532,7 @@
         and half % STEP == 0
         and local_pairs % half == 0
         and local_pairs // half % 2 == 1
+        and local_pairs // half >= half // STEP
     )
 
 

time: 304 us -> 303 us (level)
  other arithmetic: 11.4 us -> 0 us
  Pallas kernels: 291 us -> 301 us
    convert_element_type x1 -> x0, other arithmetic: 11.4 us -> none  [exchanged(): (rest.astype(jnp.float32) + left.astype(jnp.float32)).astype(jnp.bfloat16)]
    pallas_call x0 -> x1, Pallas kernels: none -> 10.6 us  [exchanged(): pl.pallas_call(add_kernel, out_shape=slab, grid=(2, halves), in_specs=[bl...]
where the time goes in v2:
time: 303 us; the launch traced here: 301 us
  Pallas kernels  301 us (99%)
    pallas_call x1, Pallas kernels, exchanged(): pl.pallas_call(functools.partial(section_kernel, count), out_shape=[slab,...  290 us
    pallas_call x1, Pallas kernels, exchanged(): pl.pallas_call(add_kernel, out_shape=slab, grid=(2, halves), in_specs=[bl...  10.6 us

profile of v2, /device:TPU:15, one launch (start us, length us, event | category | flops | bytes accessed | tf_op | source)
XLA Modules:
  0.0 300.7 jit_solution(7973049137854394389)
XLA Ops:
  0.0 290.0 %shard_map.118 = (bf16[2,5,20,32,512]{4,3,2,1,0:T(8,128)(2,1)}, bf16[2,5,20,32,512]{4,3,2,1,0:T(8,128)(2,1)}) custom-call(bf16[2,5,20,32,512]{4,3,2,1,0:T(8,128)(2,1)} %bitcast.9, bf16[64,64]{1,0:T(8,128)(2,1)} %system_real.1, bf16[64,64]{1,0:T(8,128)(2,1)} %system_imag.1, bf16[40,40]{1,0:T(8,128)(2,1)} %left_ham.1, bf16[40,40]{1,0:T(8,128)(2,1)} %left_coupling.1, ...), custom_call_target="tpu_custom_call" | custom-call | flops 10000000000 | bytes 32768000 | tf_op jit(solution)/shard_map/pallas_call | solution.py:463
  290.0 10.6 %shard_map.119 = bf16[2,5,20,32,512]{4,3,2,1,0:T(8,128)(2,1)} custom-call(bf16[2,5,20,32,512]{4,3,2,1,0:T(8,128)(2,1)} %get-tuple-element.7.rest, bf16[2,5,20,32,512]{4,3,2,1,0:T(8,128)(2,1)} %get-tuple-element.8.left), custom_call_target="tpu_custom_call" | custom-call | flops 3276800 | bytes 19660800 | tf_op jit(solution)/shard_map/pallas_call | solution.py:509

commit v3 on v2

--- a/solution.py
+++ b/solution.py
@@ -192,10 +192,9 @@
     left_damping,
     right_damping,
     energies,
-    rest_out,
+    other,
     left_out,
     mine,
-    other,
     level,
     taken,
     given,
@@ -211,7 +210,6 @@
     sys_recv,
     level_sem,
     mine_sem,
-    out_sem,
 ):
     me = lax.axis_index("rc")
     sys_index = lax.axis_index("sys")
@@ -359,6 +357,23 @@
             rows = pl.ds(pl.multiple_of(odd * half * ROWS, half * ROWS), half * ROWS)
             term = product(right_mat[block, rows, :], held) * sign
             rest[1 - part, shared, :, row, :] = term.reshape(half, ROWS, columns)
+
+    def system_rows(index):
+        swap(index).wait_recv()
+
+        @pl.loop(0, half)
+        def _(at):
+            pair = (me * halves + index) * half + at
+            damping = 0.5 * (left_damping[pair // levels] + right_damping[lax.rem(pair, levels)])
+            real, imag = mine[0, index, at], mine[1, index, at]
+            held = jnp.concatenate([real, imag, other[0, index, at], other[1, index, at]], axis=0)
+            term = product(sys_mat[...], held)
+            real, imag = real.astype(jnp.float32), imag.astype(jnp.float32)
+            energy = energies[...]
+            new_real = term[:local] + rest[0, index, at] - energy * imag - damping * real
+            new_imag = term[local:] + rest[1, index, at] + energy * real - damping * imag
+            other[0, index, at] = new_real.astype(jnp.bfloat16)
+            other[1, index, at] = new_imag.astype(jnp.bfloat16)
 
     my_sign = jnp.where(my_part == 1, 1.0, -1.0)
 
@@ -392,30 +407,16 @@
         def _(offset):
             giveback(chunk, peer(offset), me).start()
 
-    @pl.loop(0, halves)
-    def _(index):
-        swap(index).wait_recv()
-
-        @pl.loop(0, half)
-        def _(at):
-            pair = (me * halves + index) * half + at
-            damping = 0.5 * (left_damping[pair // levels] + right_damping[lax.rem(pair, levels)])
-            real, imag = mine[0, index, at], mine[1, index, at]
-            held = jnp.concatenate([real, imag, other[0, index, at], other[1, index, at]], axis=0)
-            term = product(sys_mat[...], held)
-            real, imag = real.astype(jnp.float32), imag.astype(jnp.float32)
-            energy = energies[...]
-            new_real = term[:local] + rest[0, index, at] - energy * imag - damping * real
-            new_imag = term[local:] + rest[1, index, at] + energy * real - damping * imag
-            other[0, index, at] = new_real.astype(jnp.bfloat16)
-            other[1, index, at] = new_imag.astype(jnp.bfloat16)
-
-        pltpu.make_async_copy(other.at[:, index], rest_out.at[:, index], out_sem.at[index]).start()
+        first = chunk * halves // (chunks - 1)
+        last = jnp.minimum((chunk + 1) * halves // (chunks - 1), halves)
+
+        @pl.loop(first, last)
+        def _(index):
+            system_rows(index)
 
     @pl.loop(0, halves)
     def _(index):
         swap(index).wait_send()
-        pltpu.make_async_copy(other.at[:, index], rest_out.at[:, index], out_sem.at[index]).wait()
 
     @pl.loop(0, chunks)
     def _(chunk):
@@ -429,8 +430,27 @@
             giveback(chunk, me, rank).wait_recv()
 
 
-def add_kernel(rest, left, total):
-    total[...] = (rest[...].astype(jnp.float32) + left[...].astype(jnp.float32)).astype(jnp.bfloat16)
+def add_kernel(rest, left, total, staged, sems):
+    _, halves = rest.shape[:2]
+
+    def out(part, index):
+        return pltpu.make_async_copy(
+            staged.at[part, index], total.at[part, index], sems.at[part, index]
+        )
+
+    for part in range(2):
+
+        @pl.loop(0, halves)
+        def _(index):
+            summed = rest[part, index].astype(jnp.float32) + left[part, index].astype(jnp.float32)
+            staged[part, index] = summed.astype(jnp.bfloat16)
+            out(part, index).start()
+
+    for part in range(2):
+
+        @pl.loop(0, halves)
+        def _(index):
+            out(part, index).wait()
 
 
 def exchanged(
@@ -462,11 +482,10 @@
     slab = jax.ShapeDtypeStruct(dens.shape, jnp.bfloat16)
     rest, left = pl.pallas_call(
         functools.partial(section_kernel, count),
-        out_shape=[slab, slab],
+        out_shape=[pltpu.VMEM(dens.shape, jnp.bfloat16)] * 2,
         in_specs=[anywhere] + [whole] * 8 + [scalars] * 2 + [whole],
-        out_specs=[anywhere, anywhere],
+        out_specs=[whole, whole],
         scratch_shapes=[
-            pltpu.VMEM(dens.shape, jnp.bfloat16),
             pltpu.VMEM(dens.shape, jnp.bfloat16),
             pltpu.VMEM((2, 2, half, local, columns), jnp.bfloat16),
             pltpu.VMEM((chunks, count * halves, STEP, ROWS, LANES), jnp.bfloat16),
@@ -483,10 +502,9 @@
             pltpu.SemaphoreType.DMA((halves,)),
             pltpu.SemaphoreType.DMA((3,)),
             pltpu.SemaphoreType.DMA,
-            pltpu.SemaphoreType.DMA((halves,)),
         ],
         compiler_params=pltpu.CompilerParams(
-            collective_id=0, has_side_effects=True, vmem_limit_bytes=60 * 2**20
+            collective_id=0, has_side_effects=True, vmem_limit_bytes=46 * 2**20
         ),
         cost_estimate=pl.CostEstimate(
             flops=10 * 10**9, bytes_accessed=5 * dens.size * 2, transcendentals=0
@@ -505,15 +523,18 @@
         right_damping,
         energies[None, :],
     )
-    block = pl.BlockSpec((1, 1, half, local, columns), lambda part, index: (part, index, 0, 0, 0))
     total = pl.pallas_call(
         add_kernel,
         out_shape=slab,
-        grid=(2, halves),
-        in_specs=[block, block],
-        out_specs=block,
+        in_specs=[whole, whole],
+        out_specs=anywhere,
+        scratch_shapes=[
+            pltpu.VMEM(dens.shape, jnp.bfloat16),
+            pltpu.SemaphoreType.DMA((2, halves)),
+        ],
+        compiler_params=pltpu.CompilerParams(vmem_limit_bytes=32 * 2**20),
         cost_estimate=pl.CostEstimate(
-            flops=dens.size, bytes_accessed=3 * dens.size * 2, transcendentals=0
+            flops=dens.size, bytes_accessed=dens.size * 2, transcendentals=0
         ),
     )(rest, left)
     return jnp.transpose(total.reshape(2, pairs, local, columns), (0, 2, 1, 3))
@@ -532,7 +553,7 @@
         and half % STEP == 0
         and local_pairs % half == 0
         and local_pairs // half % 2 == 1
-        and local_pairs // half >= half // STEP
+        and local_pairs // half >= half // STEP > 1
     )
 
 

time: 303 us -> 295 us (0.974)
  Pallas kernels: 301 us -> 293 us
    pallas_call x2, Pallas kernels: 301 us -> 293 us  [the longest x1 290 us: exchanged(): pl.pallas_call(functools.partial(section_kernel, count), out_shape=[pltpu...]
where the time goes in v3:
time: 295 us; the launch traced here: 293 us
  Pallas kernels  293 us (99%)
    pallas_call x1, Pallas kernels, exchanged(): pl.pallas_call(functools.partial(section_kernel, count), out_shape=[pltpu...  290 us

profile of v3, /device:TPU:15, one launch (start us, length us, event | category | flops | bytes accessed | tf_op | source)
XLA Modules:
  0.0 292.9 jit_solution(6567245880677819449)
XLA Ops:
  0.0 289.9 %shard_map.118 = (bf16[2,5,20,32,512]{4,3,2,1,0:T(8,128)(2,1)S(1)}, bf16[2,5,20,32,512]{4,3,2,1,0:T(8,128)(2,1)S(1)}) custom-call(bf16[2,5,20,32,512]{4,3,2,1,0:T(8,128)(2,1)} %bitcast.9, bf16[64,64]{1,0:T(8,128)(2,1)} %system_real.1, bf16[64,64]{1,0:T(8,128)(2,1)} %system_imag.1, bf16[40,40]{1,0:T(8,128)(2,1)} %left_ham.1, bf16[40,40]{1,0:T(8,128)(2,1)} %left_coupling.1, ...), custom_call_target="tpu_custom_call" | custom-call | flops 10000000000 | bytes 32768000 | tf_op jit(solution)/shard_map/pallas_call | solution.py:483
  289.9 3.0 %shard_map.119 = bf16[2,5,20,32,512]{4,3,2,1,0:T(8,128)(2,1)} custom-call(bf16[2,5,20,32,512]{4,3,2,1,0:T(8,128)(2,1)S(1)} %get-tuple-element.7.rest, bf16[2,5,20,32,512]{4,3,2,1,0:T(8,128)(2,1)S(1)} %get-tuple-element.8.left), custom_call_target="tpu_custom_call" | custom-call | flops 3276800 | bytes 6553600 | tf_op jit(solution)/shard_map/pallas_call | solution.py:526

commit v4 on v3

--- a/solution.py
+++ b/solution.py
@@ -10,7 +10,6 @@
 
 ROWS = 16
 LANES = 128
-STEP = 5
 
 
 def symmetric(matrix, factor):
@@ -215,17 +214,17 @@
     sys_index = lax.axis_index("sys")
     _, halves, half, local, columns = dens.shape
     levels = 2 * half
-    row_blocks, lane_blocks = local // ROWS, columns // LANES
-    chunks = half // STEP
+    row_blocks = local // ROWS
+    parts = count // (2 * row_blocks)
+    chunks = half // parts
     odd = lax.rem(me, 2)
     partner = me + 1 - 2 * odd
     shared = (halves - 1) * (1 - odd)
 
-    def task(rank):
-        part = rank // (row_blocks * lane_blocks)
-        row = lax.rem(rank // lane_blocks, row_blocks) * ROWS
-        lane = lax.rem(rank, lane_blocks) * LANES
-        return part, pl.ds(pl.multiple_of(row, ROWS), ROWS), pl.ds(pl.multiple_of(lane, LANES), LANES)
+    def task(rank, chunk):
+        part = rank // (row_blocks * parts)
+        row = lax.rem(rank // parts, row_blocks) * ROWS
+        return part, lax.rem(rank, parts) * chunks + chunk, pl.ds(pl.multiple_of(row, ROWS), ROWS)
 
     def peer(turn):
         side = count // 2
@@ -233,8 +232,8 @@
         return lax.rem(me // side + other_side, 2) * side + lax.rem(me + turn // 2, side)
 
     def part_of(rank, chunk):
-        part, row, lane = task(rank)
-        return dens.at[part, :, pl.ds(chunk * STEP, STEP), row, lane]
+        part, at, row = task(rank, chunk)
+        return dens.at[part, :, at, row, :]
 
     def forward(chunk, rank, owner):
         return pltpu.make_async_remote_copy(
@@ -252,8 +251,8 @@
         )
 
     def landing(rank, chunk):
-        part, row, lane = task(rank)
-        return left_out.at[1 - part, :, pl.ds(chunk * STEP, STEP), row, lane]
+        part, at, row = task(rank, chunk)
+        return left_out.at[1 - part, :, at, row, :]
 
     def giveback(chunk, rank, worker):
         return pltpu.make_async_remote_copy(
@@ -321,8 +320,8 @@
     def _(index):
         swap(index).start()
 
-    my_part = me // (row_blocks * lane_blocks)
-    my_row = lax.rem(me // lane_blocks, row_blocks) * ROWS
+    my_part = me // (row_blocks * parts)
+    my_row = lax.rem(me // parts, row_blocks) * ROWS
     left_mat[...] = ladder_matrix(
         left_ham[...], left_coupling[...], left_strength[...], sys_index * local + my_row
     )
@@ -387,20 +386,11 @@
 
         for side in range(2):
             held = jnp.concatenate(
-                [
-                    jnp.concatenate(
-                        [taken[chunk, 2 * number + side, at] for number in range(levels)], axis=0
-                    )
-                    for at in range(STEP)
-                ],
-                axis=1,
+                [taken[chunk, 2 * number + side] for number in range(levels)], axis=0
             )
             term = (product(left_mat[...], held) * my_sign).astype(jnp.bfloat16)
-            for at in range(STEP):
-                for number in range(levels):
-                    given[chunk, 2 * number + side, at] = term[
-                        number * ROWS : (number + 1) * ROWS, at * LANES : (at + 1) * LANES
-                    ]
+            for number in range(levels):
+                given[chunk, 2 * number + side] = term[number * ROWS : (number + 1) * ROWS]
         giveback_own(chunk).start()
 
         @pl.loop(1, count)
@@ -472,9 +462,9 @@
     half = levels // 2
     _, local, pairs, columns = density.shape
     halves = pairs // half
-    chunks = half // STEP
     size = levels * ROWS
     row_blocks = local // ROWS
+    chunks = half * 2 * row_blocks // count
     dens = jnp.transpose(density, (0, 2, 1, 3)).reshape(2, halves, half, local, columns)
     whole = pl.BlockSpec(memory_space=pltpu.VMEM)
     scalars = pl.BlockSpec(memory_space=pltpu.SMEM)
@@ -488,8 +478,8 @@
         scratch_shapes=[
             pltpu.VMEM(dens.shape, jnp.bfloat16),
             pltpu.VMEM((2, 2, half, local, columns), jnp.bfloat16),
-            pltpu.VMEM((chunks, count * halves, STEP, ROWS, LANES), jnp.bfloat16),
-            pltpu.VMEM((chunks, count * halves, STEP, ROWS, LANES), jnp.bfloat16),
+            pltpu.VMEM((chunks, count * halves, ROWS, columns), jnp.bfloat16),
+            pltpu.VMEM((chunks, count * halves, ROWS, columns), jnp.bfloat16),
             pltpu.VMEM(dens.shape, jnp.float32),
             pltpu.VMEM((size, size), jnp.bfloat16),
             pltpu.VMEM((row_blocks, size, size), jnp.bfloat16),
@@ -547,14 +537,11 @@
     if sides != 2 or levels % 2 or pairs % count or states % (2 * ROWS) or columns % LANES:
         return False
     half, local_pairs = levels // 2, pairs // count
-    tasks = 2 * (states // (2 * ROWS)) * (columns // LANES)
-    return (
-        tasks == count
-        and half % STEP == 0
-        and local_pairs % half == 0
-        and local_pairs // half % 2 == 1
-        and local_pairs // half >= half // STEP > 1
-    )
+    row_parts = 2 * (states // (2 * ROWS))
+    if count % row_parts or half % (count // row_parts) or local_pairs % half:
+        return False
+    halves, chunks = local_pairs // half, half * row_parts // count
+    return halves % 2 == 1 and halves >= chunks > 1
 
 
 def solution(mesh):

time: 295 us -> 296 us (level)
  no operation moved by 1% of the time
where the time goes in v4:
time: 296 us; the launch traced here: 293 us
  Pallas kernels  293 us (99%)
    pallas_call x1, Pallas kernels, exchanged(): pl.pallas_call(functools.partial(section_kernel, count), out_shape=[pltpu...  291 us

profile of v4, /device:TPU:15, one launch (start us, length us, event | category | flops | bytes accessed | tf_op | source)
XLA Modules:
  0.0 293.5 jit_solution(4121365319260874373)
XLA Ops:
  0.0 290.5 %shard_map.118 = (bf16[2,5,20,32,512]{4,3,2,1,0:T(8,128)(2,1)S(1)}, bf16[2,5,20,32,512]{4,3,2,1,0:T(8,128)(2,1)S(1)}) custom-call(bf16[2,5,20,32,512]{4,3,2,1,0:T(8,128)(2,1)} %bitcast.9, bf16[64,64]{1,0:T(8,128)(2,1)} %system_real.1, bf16[64,64]{1,0:T(8,128)(2,1)} %system_imag.1, bf16[40,40]{1,0:T(8,128)(2,1)} %left_ham.1, bf16[40,40]{1,0:T(8,128)(2,1)} %left_coupling.1, ...), custom_call_target="tpu_custom_call" | custom-call | flops 10000000000 | bytes 32768000 | tf_op jit(solution)/shard_map/pallas_call | solution.py:473
  290.5 3.0 %shard_map.119 = bf16[2,5,20,32,512]{4,3,2,1,0:T(8,128)(2,1)} custom-call(bf16[2,5,20,32,512]{4,3,2,1,0:T(8,128)(2,1)S(1)} %get-tuple-element.7.rest, bf16[2,5,20,32,512]{4,3,2,1,0:T(8,128)(2,1)S(1)} %get-tuple-element.8.left), custom_call_target="tpu_custom_call" | custom-call | flops 3276800 | bytes 6553600 | tf_op jit(solution)/shard_map/pallas_call | solution.py:516

commit v5 on v4

--- a/solution.py
+++ b/solution.py
@@ -10,6 +10,7 @@
 
 ROWS = 16
 LANES = 128
+AHEAD = 2
 
 
 def symmetric(matrix, factor):
@@ -306,8 +307,7 @@
     mine_copy = pltpu.make_async_copy(dens, mine, mine_sem)
     mine_copy.start()
 
-    @pl.loop(0, chunks)
-    def _(chunk):
+    def send(chunk):
         forward_own(chunk).start()
 
         @pl.loop(1, count)
@@ -316,9 +316,9 @@
 
         swap(chunk).start()
 
-    @pl.loop(chunks, halves)
-    def _(index):
-        swap(index).start()
+    @pl.loop(0, AHEAD)
+    def _(chunk):
+        send(chunk)
 
     my_part = me // (row_blocks * parts)
     my_row = lax.rem(me // parts, row_blocks) * ROWS
@@ -384,6 +384,10 @@
         def _(offset):
             forward(chunk, me, peer(offset)).wait_recv()
 
+        @pl.when(chunk + AHEAD < chunks)
+        def _():
+            send(chunk + AHEAD)
+
         for side in range(2):
             held = jnp.concatenate(
                 [taken[chunk, 2 * number + side] for number in range(levels)], axis=0
@@ -397,12 +401,17 @@
         def _(offset):
             giveback(chunk, peer(offset), me).start()
 
-        first = chunk * halves // (chunks - 1)
-        last = jnp.minimum((chunk + 1) * halves // (chunks - 1), halves)
-
-        @pl.loop(first, last)
-        def _(index):
-            system_rows(index)
+        @pl.when(chunk > 0)
+        def _():
+            system_rows(chunk - 1)
+
+    @pl.loop(chunks, halves)
+    def _(index):
+        swap(index).start()
+
+    @pl.loop(chunks - 1, halves)
+    def _(index):
+        system_rows(index)
 
     @pl.loop(0, halves)
     def _(index):
@@ -541,7 +550,7 @@
     if count % row_parts or half % (count // row_parts) or local_pairs % half:
         return False
     halves, chunks = local_pairs // half, half * row_parts // count
-    return halves % 2 == 1 and halves >= chunks > 1
+    return halves % 2 == 1 and halves >= chunks >= AHEAD
 
 
 def solution(mesh):

time: 296 us -> 296 us (level)
  no operation moved by 1% of the time
where the time goes in v5:
time: 296 us; the launch traced here: 294 us
  Pallas kernels  294 us (99%)
    pallas_call x1, Pallas kernels, exchanged(): pl.pallas_call(functools.partial(section_kernel, count), out_shape=[pltpu...  291 us

profile of v5, /device:TPU:15, one launch (start us, length us, event | category | flops | bytes accessed | tf_op | source)
XLA Modules:
  0.0 293.6 jit_solution(5293745014479520134)
XLA Ops:
  0.0 290.6 %shard_map.118 = (bf16[2,5,20,32,512]{4,3,2,1,0:T(8,128)(2,1)S(1)}, bf16[2,5,20,32,512]{4,3,2,1,0:T(8,128)(2,1)S(1)}) custom-call(bf16[2,5,20,32,512]{4,3,2,1,0:T(8,128)(2,1)} %bitcast.9, bf16[64,64]{1,0:T(8,128)(2,1)} %system_real.1, bf16[64,64]{1,0:T(8,128)(2,1)} %system_imag.1, bf16[40,40]{1,0:T(8,128)(2,1)} %left_ham.1, bf16[40,40]{1,0:T(8,128)(2,1)} %left_coupling.1, ...), custom_call_target="tpu_custom_call" | custom-call | flops 10000000000 | bytes 32768000 | tf_op jit(solution)/shard_map/pallas_call | solution.py:482
  290.6 3.0 %shard_map.119 = bf16[2,5,20,32,512]{4,3,2,1,0:T(8,128)(2,1)} custom-call(bf16[2,5,20,32,512]{4,3,2,1,0:T(8,128)(2,1)S(1)} %get-tuple-element.7.rest, bf16[2,5,20,32,512]{4,3,2,1,0:T(8,128)(2,1)S(1)} %get-tuple-element.8.left), custom_call_target="tpu_custom_call" | custom-call | flops 3276800 | bytes 6553600 | tf_op jit(solution)/shard_map/pallas_call | solution.py:525

commit v6 on v5

--- a/solution.py
+++ b/solution.py
@@ -10,6 +10,7 @@
 
 ROWS = 16
 LANES = 128
+PIECE = 2
 AHEAD = 2
 
 
@@ -280,6 +281,17 @@
             device_id_type=pl.DeviceIdType.MESH,
         )
 
+    def swap_piece(index, piece):
+        held = (slice(None), index, pl.ds(piece * PIECE, PIECE))
+        return pltpu.make_async_remote_copy(
+            src_ref=dens.at[held],
+            dst_ref=other.at[held],
+            send_sem=sys_send.at[index],
+            recv_sem=sys_recv.at[index],
+            device_id={"sys": 1 - sys_index},
+            device_id_type=pl.DeviceIdType.MESH,
+        )
+
     barrier = pltpu.get_barrier_semaphore()
 
     @pl.loop(1, count)
@@ -314,7 +326,9 @@
         def _(offset):
             forward(chunk, peer(offset), me).start()
 
-        swap(chunk).start()
+            @pl.when(offset <= half // PIECE)
+            def _():
+                swap_piece(chunk, offset - 1).start()
 
     @pl.loop(0, AHEAD)
     def _(chunk):
@@ -547,6 +561,8 @@
         return False
     half, local_pairs = levels // 2, pairs // count
     row_parts = 2 * (states // (2 * ROWS))
+    if half % PIECE or half // PIECE >= count:
+        return False
     if count % row_parts or half % (count // row_parts) or local_pairs % half:
         return False
     halves, chunks = local_pairs // half, half * row_parts // count

time: 296 us -> 296 us (level)
  no operation moved by 1% of the time
where the time goes in v6:
time: 296 us; the launch traced here: 294 us
  Pallas kernels  294 us (99%)
    pallas_call x1, Pallas kernels, exchanged(): pl.pallas_call(functools.partial(section_kernel, count), out_shape=[pltpu...  291 us

profile of v6, /device:TPU:15, one launch (start us, length us, event | category | flops | bytes accessed | tf_op | source)
XLA Modules:
  0.0 293.6 jit_solution(14936180885014442067)
XLA Ops:
  0.0 290.6 %shard_map.118 = (bf16[2,5,20,32,512]{4,3,2,1,0:T(8,128)(2,1)S(1)}, bf16[2,5,20,32,512]{4,3,2,1,0:T(8,128)(2,1)S(1)}) custom-call(bf16[2,5,20,32,512]{4,3,2,1,0:T(8,128)(2,1)} %bitcast.9, bf16[64,64]{1,0:T(8,128)(2,1)} %system_real.1, bf16[64,64]{1,0:T(8,128)(2,1)} %system_imag.1, bf16[40,40]{1,0:T(8,128)(2,1)} %left_ham.1, bf16[40,40]{1,0:T(8,128)(2,1)} %left_coupling.1, ...), custom_call_target="tpu_custom_call" | custom-call | flops 10000000000 | bytes 32768000 | tf_op jit(solution)/shard_map/pallas_call | solution.py:496
  290.6 3.0 %shard_map.119 = bf16[2,5,20,32,512]{4,3,2,1,0:T(8,128)(2,1)} custom-call(bf16[2,5,20,32,512]{4,3,2,1,0:T(8,128)(2,1)S(1)} %get-tuple-element.7.rest, bf16[2,5,20,32,512]{4,3,2,1,0:T(8,128)(2,1)S(1)} %get-tuple-element.8.left), custom_call_target="tpu_custom_call" | custom-call | flops 3276800 | bytes 6553600 | tf_op jit(solution)/shard_map/pallas_call | solution.py:539

commit v7 on v6

--- a/solution.py
+++ b/solution.py
@@ -193,13 +193,13 @@
     left_damping,
     right_damping,
     energies,
-    other,
+    rest,
     left_out,
     mine,
+    other,
     level,
     taken,
     given,
-    rest,
     left_mat,
     right_mat,
     sys_mat,
@@ -305,6 +305,21 @@
     )
     pl.semaphore_wait(barrier, count)
 
+    def send(chunk):
+        forward_own(chunk).start()
+
+        @pl.loop(1, count)
+        def _(offset):
+            forward(chunk, peer(offset), me).start()
+
+            @pl.when(offset <= half // PIECE)
+            def _():
+                swap_piece(chunk, offset - 1).start()
+
+    @pl.loop(0, AHEAD)
+    def _(chunk):
+        send(chunk)
+
     level_copy = pltpu.make_async_remote_copy(
         src_ref=dens.at[:, shared],
         dst_ref=level.at[:, odd],
@@ -318,21 +333,6 @@
     level_own.start()
     mine_copy = pltpu.make_async_copy(dens, mine, mine_sem)
     mine_copy.start()
-
-    def send(chunk):
-        forward_own(chunk).start()
-
-        @pl.loop(1, count)
-        def _(offset):
-            forward(chunk, peer(offset), me).start()
-
-            @pl.when(offset <= half // PIECE)
-            def _():
-                swap_piece(chunk, offset - 1).start()
-
-    @pl.loop(0, AHEAD)
-    def _(chunk):
-        send(chunk)
 
     my_part = me // (row_blocks * parts)
     my_row = lax.rem(me // parts, row_blocks) * ROWS
@@ -385,8 +385,8 @@
             energy = energies[...]
             new_real = term[:local] + rest[0, index, at] - energy * imag - damping * real
             new_imag = term[local:] + rest[1, index, at] + energy * real - damping * imag
-            other[0, index, at] = new_real.astype(jnp.bfloat16)
-            other[1, index, at] = new_imag.astype(jnp.bfloat16)
+            rest[0, index, at] = new_real
+            rest[1, index, at] = new_imag
 
     my_sign = jnp.where(my_part == 1, 1.0, -1.0)
 
@@ -455,7 +455,7 @@
 
         @pl.loop(0, halves)
         def _(index):
-            summed = rest[part, index].astype(jnp.float32) + left[part, index].astype(jnp.float32)
+            summed = rest[part, index] + left[part, index].astype(jnp.float32)
             staged[part, index] = summed.astype(jnp.bfloat16)
             out(part, index).start()
 
@@ -495,15 +495,18 @@
     slab = jax.ShapeDtypeStruct(dens.shape, jnp.bfloat16)
     rest, left = pl.pallas_call(
         functools.partial(section_kernel, count),
-        out_shape=[pltpu.VMEM(dens.shape, jnp.bfloat16)] * 2,
+        out_shape=[
+            pltpu.VMEM(dens.shape, jnp.float32),
+            pltpu.VMEM(dens.shape, jnp.bfloat16),
+        ],
         in_specs=[anywhere] + [whole] * 8 + [scalars] * 2 + [whole],
         out_specs=[whole, whole],
         scratch_shapes=[
             pltpu.VMEM(dens.shape, jnp.bfloat16),
+            pltpu.VMEM(dens.shape, jnp.bfloat16),
             pltpu.VMEM((2, 2, half, local, columns), jnp.bfloat16),
             pltpu.VMEM((chunks, count * halves, ROWS, columns), jnp.bfloat16),
             pltpu.VMEM((chunks, count * halves, ROWS, columns), jnp.bfloat16),
-            pltpu.VMEM(dens.shape, jnp.float32),
             pltpu.VMEM((size, size), jnp.bfloat16),
             pltpu.VMEM((row_blocks, size, size), jnp.bfloat16),
             pltpu.VMEM((2 * local, 4 * local), jnp.bfloat16),
@@ -517,7 +520,7 @@
             pltpu.SemaphoreType.DMA,
         ],
         compiler_params=pltpu.CompilerParams(
-            collective_id=0, has_side_effects=True, vmem_limit_bytes=46 * 2**20
+            collective_id=0, has_side_effects=True, vmem_limit_bytes=41 * 2**20
         ),
         cost_estimate=pl.CostEstimate(
             flops=10 * 10**9, bytes_accessed=5 * dens.size * 2, transcendentals=0

time: 296 us -> 305 us (1.030)
  local copies, waits for them, and re-layouts: 0 us -> 9.38 us
    unnamed x0 -> x4, local copies, waits for them, and re-layouts: none -> 9.38 us
where the time goes in v7:
time: 305 us; the launch traced here: 303 us
  Pallas kernels  293 us (96%)
  local copies, waits for them, and re-layouts  9.38 us (3%)
    pallas_call x1, Pallas kernels, exchanged(): pl.pallas_call(functools.partial(section_kernel, count), out_shape=[pltpu...  290 us
    unnamed x4, local copies, waits for them, and re-layouts  9.38 us

profile of v7, /device:TPU:15, one launch (start us, length us, event | category | flops | bytes accessed | tf_op | source)
XLA Modules:
  0.0 302.8 jit_solution(4554754580348803098)
XLA Ops:
  0.0 290.5 %shard_map.118 = (f32[2,5,20,32,512]{4,3,2,1,0:T(8,128)S(1)}, bf16[2,5,20,32,512]{4,3,2,1,0:T(8,128)(2,1)S(1)}) custom-call(bf16[2,5,20,32,512]{4,3,2,1,0:T(8,128)(2,1)} %bitcast.9, bf16[64,64]{1,0:T(8,128)(2,1)} %system_real.1, bf16[64,64]{1,0:T(8,128)(2,1)} %system_imag.1, bf16[40,40]{1,0:T(8,128)(2,1)} %left_ham.1, bf16[40,40]{1,0:T(8,128)(2,1)} %left_coupling.1, ...), custom_call_target="tpu_custom_call" | custom-call | flops 10000000000 | bytes 32768000 | tf_op jit(solution)/shard_map/pallas_call | solution.py:496
  290.5 0.0 copy-start
  290.5 4.7 %copy-done = f32[2,5,20,32,512]{4,3,2,1,0:T(8,128)} copy-done((f32[2,5,20,32,512]{4,3,2,1,0:T(8,128)}, f32[2,5,20,32,512]{4,3,2,1,0:T(8,128)S(1)}, u32[]{:S(2)}) %copy-start) | copy-done | bytes 13107224
  295.2 0.0 copy-start.1
  295.2 4.7 %copy-done.1 = f32[2,5,20,32,512]{4,3,2,1,0:T(8,128)S(1)} copy-done((f32[2,5,20,32,512]{4,3,2,1,0:T(8,128)S(1)}, f32[2,5,20,32,512]{4,3,2,1,0:T(8,128)}, u32[]{:S(2)}) %copy-start.1) | copy-done | bytes 13107224
  299.9 2.9 shard_map.119
Async XLA Ops:
  290.5 4.7 %copy-start = (f32[2,5,20,32,512]{4,3,2,1,0:T(8,128)}, f32[2,5,20,32,512]{4,3,2,1,0:T(8,128)S(1)}, u32[]{:S(2)}) copy-start(f32[2,5,20,32,512]{4,3,2,1,0:T(8,128)S(1)} %get-tuple-element.7.rest) | copy-start | bytes 39321604
  295.2 4.7 %copy-start.1 = (f32[2,5,20,32,512]{4,3,2,1,0:T(8,128)S(1)}, f32[2,5,20,32,512]{4,3,2,1,0:T(8,128)}, u32[]{:S(2)}) copy-start(f32[2,5,20,32,512]{4,3,2,1,0:T(8,128)} %copy-done) | copy-start | bytes 39321604

commit v8 on v7

--- a/solution.py
+++ b/solution.py
@@ -548,7 +548,7 @@
             pltpu.VMEM(dens.shape, jnp.bfloat16),
             pltpu.SemaphoreType.DMA((2, halves)),
         ],
-        compiler_params=pltpu.CompilerParams(vmem_limit_bytes=32 * 2**20),
+        compiler_params=pltpu.CompilerParams(vmem_limit_bytes=12 * 2**20),
         cost_estimate=pl.CostEstimate(
             flops=dens.size, bytes_accessed=dens.size * 2, transcendentals=0
         ),

time: 305 us -> 296 us (0.970)
  local copies, waits for them, and re-layouts: 9.38 us -> 0 us
    unnamed x4 -> x0, local copies, waits for them, and re-layouts: 9.38 us -> none
where the time goes in v8:
time: 296 us; the launch traced here: 293 us
  Pallas kernels  293 us (99%)
    pallas_call x1, Pallas kernels, exchanged(): pl.pallas_call(functools.partial(section_kernel, count), out_shape=[pltpu...  290 us

profile of v8, /device:TPU:15, one launch (start us, length us, event | category | flops | bytes accessed | tf_op | source)
XLA Modules:
  0.0 293.4 jit_solution(12926427154692483150)
XLA Ops:
  0.0 290.5 %shard_map.118 = (f32[2,5,20,32,512]{4,3,2,1,0:T(8,128)S(1)}, bf16[2,5,20,32,512]{4,3,2,1,0:T(8,128)(2,1)S(1)}) custom-call(bf16[2,5,20,32,512]{4,3,2,1,0:T(8,128)(2,1)} %bitcast.9, bf16[64,64]{1,0:T(8,128)(2,1)} %system_real.1, bf16[64,64]{1,0:T(8,128)(2,1)} %system_imag.1, bf16[40,40]{1,0:T(8,128)(2,1)} %left_ham.1, bf16[40,40]{1,0:T(8,128)(2,1)} %left_coupling.1, ...), custom_call_target="tpu_custom_call" | custom-call | flops 10000000000 | bytes 32768000 | tf_op jit(solution)/shard_map/pallas_call | solution.py:496
  290.5 2.9 %shard_map.119 = bf16[2,5,20,32,512]{4,3,2,1,0:T(8,128)(2,1)} custom-call(f32[2,5,20,32,512]{4,3,2,1,0:T(8,128)S(1)} %get-tuple-element.7.rest, bf16[2,5,20,32,512]{4,3,2,1,0:T(8,128)(2,1)S(1)} %get-tuple-element.8.left), custom_call_target="tpu_custom_call" | custom-call | flops 3276800 | bytes 6553600 | tf_op jit(solution)/shard_map/pallas_call | solution.py:542
